TPU v7x, 128 devices: a whole 4x4x4 slice. The times are simulated.
128 devices in a mesh: kv: 16 (over x, z), tp: 8 (over y, core).
Axes of the slice: x: 4, y: 4, z: 4, core: 2. Of those that a mesh axis runs over, the one named last changes fastest.
Arguments:
- queries: bfloat16 [16, 16384], P('kv', 'tp'), may hold values from -16 to 16
- sign_bits: int32 [128], replicated, may hold values from 0 to 1
- key_pages: bfloat16 [512, 256, 1024], P('kv', None, 'tp'), may hold values from -16 to 16
- value_pages: bfloat16 [512, 256, 1024], P('kv', None, 'tp'), may hold values from -6 to 6
- page_table: int32 [16, 16, 4], P('kv'), may hold values from 0 to 31, as said below
- page_count: int32 [16, 16], P('kv'), may hold values from 0 to 4, as said below
- residual: bfloat16 [16, 16384], P(None, 'tp'), may hold values from -8 to 8
- norm_gain: bfloat16 [16384], P('tp'), may hold values from 0.099609375 to 1.8984375
- gate_weight: bfloat16 [16384, 26624], P('tp', 'kv'), may hold values from -0.046875 to 0.046875
- up_weight: bfloat16 [16384, 26624], P('tp', 'kv'), may hold values from -0.046875 to 0.046875
- down_weight: bfloat16 [26624, 16384], P('kv', 'tp'), may hold values from -0.0390625 to 0.0390625
Outputs:
- layer_out: bfloat16 [16, 16384], P('kv', 'tp')
Inputs may be any that keep to these rules, and one draw needn't show every extreme that they name: `page_count`: on each device one request holds exactly 4 pages; every request owns at least one page on some device; a device's live pages number at most 32 and some pool pages may be owned by nobody. `page_table`: live entries of one device are distinct pool pages; entries past a list's count are arbitrary pool pages.
All inputs are finite; a program needn't handle non-finite values.
Results may differ from a plain program's by a relative error of at most 0.019.
Values may be sent and summed in bfloat16 or wider, within the bound.
A program may use at most 128 MiB of HBM per device.

v0:
```python
from functools import partial

import jax
import jax.numpy as jnp
from jax import lax
from jax.sharding import PartitionSpec as P

fill_value = -1e30
epsilon = 1e-05


def joined(value, axis, join):
    pieces = jax.tree.map(lambda part: lax.all_gather(part, axis), value)
    head = jax.tree.map(lambda part: part[0], pieces)
    tail = jax.tree.map(lambda part: part[1:], pieces)
    running, _ = lax.scan(lambda running, piece: (join(running, piece), None), head, tail)
    return running


def sylvester(size):
    index = jnp.arange(size, dtype=jnp.int32)
    common = jnp.bitwise_and(index[:, None], index[None, :])
    parity = jnp.zeros((size, size), jnp.int32)
    for level in range(size.bit_length() - 1):
        parity = parity + jnp.bitwise_and(jnp.right_shift(common, level), 1)
    return (1 - 2 * (parity % 2)).astype(jnp.float32)


def rotate(queries, sign_bits):
    head_size = sign_bits.shape[0]
    signs = (1 - 2 * sign_bits).astype(jnp.bfloat16)
    heads_here = queries.shape[1] // head_size
    signed = queries.reshape(queries.shape[0], heads_here, head_size) * signs
    turned = jnp.einsum(
        "nhd,de->nhe",
        signed,
        sylvester(head_size).astype(jnp.bfloat16),
        preferred_element_type=jnp.float32,
    )
    return (
        (turned / head_size).astype(jnp.bfloat16).reshape(queries.shape[0], heads_here * head_size)
    )


def request_partials(key_pages, value_pages, head_size, items):
    query_row, page_list, live_count = items
    groups = key_pages.shape[2] // head_size
    slots = page_list.shape[0]
    page_keys = key_pages[page_list].reshape(slots, key_pages.shape[1], groups, head_size)
    page_values = value_pages[page_list].reshape(slots, value_pages.shape[1], groups, head_size)
    query_heads = query_row.reshape(groups, -1, head_size)
    scores = jnp.einsum(
        "gqd,jtgd->jgqt", query_heads, page_keys, preferred_element_type=jnp.float32
    )
    page_max = jnp.max(scores, axis=-1)
    weights = jnp.exp(scores - page_max[..., None]).astype(jnp.bfloat16)
    page_total = jnp.sum(weights.astype(jnp.float32), axis=-1)
    page_out = jnp.einsum(
        "jgqt,jtgd->jgqd", weights, page_values, preferred_element_type=jnp.float32
    )
    alive = (jnp.arange(slots, dtype=jnp.int32) < live_count)[:, None, None]
    masked = jnp.where(alive, page_max, fill_value)
    best = jnp.max(masked, axis=0)
    factor = jnp.where(alive, jnp.exp(masked - best), 0.0)
    return (
        best,
        jnp.sum(factor * page_total, axis=0),
        jnp.sum(factor[..., None] * page_out, axis=0),
    )


def join_partials(first, second):
    best = jnp.maximum(first[0], second[0])
    first_factor = jnp.exp(first[0] - best)
    second_factor = jnp.exp(second[0] - best)
    total = first_factor * first[1] + second_factor * second[1]
    merged = first_factor[..., None] * first[2] + second_factor[..., None] * second[2]
    return (best, total, merged)


def activate(gate_sum, upper_sum, square_sum, features):
    inverse = lax.rsqrt(square_sum / features + epsilon)[:, None]
    return (jax.nn.silu(gate_sum * inverse) * (upper_sum * inverse)).astype(jnp.bfloat16)


def shards(
    queries,
    sign_bits,
    key_pages,
    value_pages,
    page_table,
    page_count,
    residual,
    norm_gain,
    gate_weight,
    up_weight,
    down_weight,
):
    head_size = sign_bits.shape[0]
    rotated = rotate(queries, sign_bits)
    page_list = page_table[0]
    live_count = page_count[0]
    requests = page_list.shape[0]
    groups = key_pages.shape[2] // head_size
    per_group = rotated.shape[1] // head_size // groups
    start_best = jnp.full((requests, groups, per_group), fill_value, jnp.float32)
    start_total = jnp.zeros((requests, groups, per_group), jnp.float32)
    start_merged = jnp.zeros((requests, groups, per_group, head_size), jnp.float32)
    per_request = partial(request_partials, key_pages, value_pages, head_size)
    start = jnp.int32(0)
    best, total, merged = lax.map(
        per_request,
        (lax.all_gather(rotated, "kv", axis=0, tiled=True), page_list, live_count),
        batch_size=8,
    )
    best, total, merged = (
        lax.dynamic_update_slice_in_dim(start_best, best, start, 0),
        lax.dynamic_update_slice_in_dim(start_total, total, start, 0),
        lax.dynamic_update_slice_in_dim(start_merged, merged, start, 0),
    )
    best, total, merged = joined((best, total, merged), "kv", join_partials)
    attention = (
        (merged / total[..., None])
        .astype(jnp.bfloat16)
        .reshape(requests, groups * per_group * head_size)
    )
    stream = residual.astype(jnp.float32) + attention.astype(jnp.float32)
    squares = jnp.sum(stream * stream, axis=-1)
    scaled = (stream * norm_gain.astype(jnp.float32)).astype(jnp.bfloat16)
    gate_part = jnp.dot(scaled, gate_weight, preferred_element_type=jnp.float32)
    upper_part = jnp.dot(scaled, up_weight, preferred_element_type=jnp.float32)
    features = residual.shape[1] * lax.axis_size("tp")
    gate_sum, upper_sum, square_sum = lax.psum((gate_part, upper_part, squares), "tp")
    hidden = activate(gate_sum, upper_sum, square_sum, features)
    share = requests // lax.axis_size("kv")
    mixed = lax.psum_scatter(
        jnp.dot(hidden, down_weight, preferred_element_type=jnp.float32).astype(jnp.bfloat16),
        "kv",
        scatter_dimension=0,
        tiled=True,
    ).astype(jnp.float32)
    own_stream = lax.dynamic_slice_in_dim(stream, lax.axis_index("kv") * share, share, 0)
    return (own_stream + mixed).astype(jnp.bfloat16)


def solution(mesh):
    in_specs = (
        P("kv", "tp"),
        P(),
        P("kv", None, "tp"),
        P("kv", None, "tp"),
        P("kv", None, None),
        P("kv", None),
        P(None, "tp"),
        P("tp"),
        P("tp", "kv"),
        P("tp", "kv"),
        P("kv", "tp"),
    )
    out_specs = P("kv", "tp")
    return jax.shard_map(shards, mesh=mesh, in_specs=in_specs, out_specs=out_specs, check_vma=False)
```

profile of v0, /device:TPU:1, one launch (start us, length us, event | category | flops | bytes accessed | tf_op | source)
XLA Modules:
  0.0 272.7 jit_solution(9058249955984881264)
XLA Ops:
  6.5 0.6 broadcast.168
  7.1 1.4 reduce.12
  8.6 0.8 reshape_squeeze.7
  9.3 0.7 subtract_convert_fusion
  10.0 0.7 reduce.9
  10.9 20.5 %all-gather = bf16[16,1,2048]{2,1,0:T(2,128)(2,1)S(1)} all-gather(bf16[1,1,2048]{2,1,0:T(2,128)(2,1)S(1)} %reshape.191), channel_id=1, replica_groups=mesh['kv'=16,'tp'=8] {'kv'}, dimensions={0}, use_global_device_ids=true | all-gather | bytes 69632 | tf_op jit(solution)/shard_map/all_gather | solution.py:113
  31.6 14.3 %while.28 = (s32[]{:T(128)}, f32[2,8,1,16]{3,1,2,0:T(8,128)S(1)}, f32[2,8,1,16]{3,1,2,0:T(8,128)S(1)}, f32[2,8,1,16,128]{4,3,2,1,0:T(8,128)S(1)}, s32[2,8]{1,0:T...) while((s32[]{:T(128)}, f32[2,8,1,16]{3,1,2,0:T(8,128)S(1)}, ...), condition=%wide.region_6.7_spmd, body=%wide.region_0.6_spmd.sunk | while | flops 68144512 | bytes 14492865 | solution.py:111
  31.8 2.5 gather_fusion
  34.3 0.7 fusion.51
  35.1 0.3 convert_reduce_fusion.2
  35.7 2.5 gather_fusion.1
  38.2 0.4 fusion.53
  38.9 2.5 gather_fusion
  41.5 0.7 fusion.51
  42.2 0.3 convert_reduce_fusion.2
  42.8 2.5 gather_fusion.1
  45.4 0.4 fusion.53
  45.9 0.6 copy-done
  46.6 17.3 %all_gather.13 = f32[16,16,1,16]{3,1,2,0:T(8,128)S(1)} all-gather(f32[1,16,1,16]{3,1,2,0:T(8,128)S(1)} %bitcast.155), channel_id=1, replica_groups=mesh['kv'=16,'tp'=8] {'kv'}, dimensions={0}, use_global_device_ids=true | all-gather | bytes 17408 | tf_op jit(solution)/shard_map/all_gather | solution.py:13
  63.9 16.8 %all_gather.14 = f32[16,16,1,16]{3,1,2,0:T(8,128)S(1)} all-gather(f32[1,16,1,16]{3,1,2,0:T(8,128)S(1)} %bitcast.156), channel_id=1, replica_groups=mesh['kv'=16,'tp'=8] {'kv'}, dimensions={0}, use_global_device_ids=true | all-gather | bytes 17408 | tf_op jit(solution)/shard_map/all_gather | solution.py:13
  80.7 15.1 %all-gather.3.cloned.1.call-done = f32[16,16,1,16,128]{4,3,2,1,0:T(8,128)} async-done(((f32[1,16,1,16,128]{4,3,2,1,0:T(8,128)}), f32[16,16,1,16,128]{4,3,2,1,0:T(8,128)}) %all-gather.3.cloned.1.call-update) | async-done | bytes 2097168 | tf_op jit(solution)/shard_map/all_gather | solution.py:13
  95.7 0.9 slice_bitcast_fusion.1
  96.6 1.7 slice_bitcast_fusion
  98.4 3.3 %while.29 = (s32[]{:T(128)}, f32[16,1,16]{2,1,0:T(1,128)S(1)}, f32[16,1,16]{2,1,0:T(1,128)S(1)}, f32[16,1,16,128]{3,2,1,0:T(8,128)S(1)}, f32[15,16,1,16]{3,1,2,0...) while((s32[]{:T(128)}, f32[16,1,16]{2,1,0:T(1,128)S(1)}, ...), condition=%wide.region_8.9_spmd, body=%wide.region_7.8_spmd.sunk | while | flops 99842 | bytes 407653 | solution.py:16
  102.0 4.6 %fusion.22 = f32[16,1664]{1,0:T(8,128)} fusion(bf16[2048,1664]{1,0:T(8,128)(2,1)} %param.24, f32[16,2048]{1,0:T(8,128)S(1)} %get-tuple-element.172, f32[2048]{0:T(1024)S(1)} %convert_element_type.57), kind=kOutput, calls=%fused_computation.59 | convolution fusion | flops 109117440 | bytes 7061504 | tf_op jit(solution)/shard_map/dot_general | solution.py:131
  106.6 4.6 %fusion.23 = f32[16,1664]{1,0:T(8,128)} fusion(bf16[2048,1664]{1,0:T(8,128)(2,1)} %param.23, f32[16,2048]{1,0:T(8,128)S(1)} %get-tuple-element.172, f32[2048]{0:T(1024)S(1)} %convert_element_type.57), kind=kOutput, calls=%fused_computation.60 | convolution fusion | flops 109117440 | bytes 7061504 | tf_op jit(solution)/shard_map/dot_general | solution.py:130
  111.2 13.4 %psum.22 = f32[16]{0:T(128)S(1)} all-reduce(f32[16]{0:T(128)S(1)} %get-tuple-element.171), channel_id=1, replica_groups=mesh['kv'=16,'tp'=8] {'tp'}, use_global_device_ids=true, to_apply=%region_11.12 | all-reduce | flops 16 | bytes 128 | tf_op jit(solution)/shard_map/psum | solution.py:133
  124.6 55.6 %all-reduce.7.cloned.1.call-done = (f32[16,1664]{1,0:T(8,128)}, f32[16,1664]{1,0:T(8,128)}) async-done(((f32[16,1664]{1,0:T(8,128)}, f32[16,1664]{1,0:T(8,128)}), (f32[16,1664]{1,0:T(8,128)}, f32[16,1664]{1,0:T(8,128)})) %all-reduce.7.cloned.1.call-update) | async-done | bytes 213008 | tf_op jit(solution)/shard_map/psum | solution.py:133
  180.2 4.7 %convolution_convert_fusion = bf16[16,2048]{1,0:T(8,128)(2,1)} fusion(bf16[1664,2048]{1,0:T(8,128)(2,1)} %param.25, f32[16,1664]{1,0:T(8,128)} %get-tuple-element.163, f32[16,1664]{1,0:T(8,128)} %get-tuple-element.164, f32[16]{0:T(128)S(1)} %add_rsqrt_fusion), kind=kOutput, calls=%fused_computation.30 | convolution fusion | flops 109297664 | bytes 7094336 | tf_op jit(solution)/shard_map/dot_general | solution.py:137
  185.0 0.6 dynamic-slice
  185.6 78.5 %all-reduce.5.cloned.1.call-done = bf16[16,2048]{1,0:T(8,128)(2,1)} async-done(((bf16[16,2048]{1,0:T(8,128)(2,1)}), bf16[16,2048]{1,0:T(8,128)(2,1)}) %all-reduce.5.cloned.1.call-update) | async-done | bytes 65552
  264.2 2.0 fusion.25
  (97 shorter events, 4.6 us)
Async XLA Ops:
  6.5 89.2 %all-gather.3.cloned.1.call-start = ((), (), s32[]{:S(2)}) async-start(), calls=%async_computation | async-start | bytes 2228224 | tf_op jit(solution)/shard_map/all_gather | solution.py:13
  31.5 49.1 %copy-start.2 = (bf16[2048]{0:T(1024)(128)(2,1)S(1)}, bf16[2048]{0:T(1024)(128)(2,1)}, u32[]{:S(2)}) copy-start(bf16[2048]{0:T(1024)(128)(2,1)} %param.22) | copy-start | bytes 12292
  45.9 0.7 copy-start
  46.5 133.7 %all-reduce.7.cloned.1.call-start = ((), (), s32[]{:S(2)}) async-start(), calls=%async_computation.2 | async-start | bytes 425984 | tf_op jit(solution)/shard_map/psum | solution.py:133
  98.4 3.5 %copy-start.1 = (bf16[16,2048]{1,0:T(8,128)(2,1)S(1)}, bf16[16,2048]{1,0:T(8,128)(2,1)}, u32[]{:S(2)}) copy-start(bf16[16,2048]{1,0:T(8,128)(2,1)} %param.21) | copy-start | bytes 196612
  124.5 139.6 %all-reduce.5.cloned.1.call-start = ((), (), s32[]{:S(2)}) async-start(), calls=%async_computation.1 | async-start | bytes 131072
  180.2 4.8 %copy-start.3 = (u32[128]{0:T(128)S(1)}, u32[128]{0:T(128)}, u32[]{:S(2)}) copy-start(u32[128]{0:T(128)} %constant.92) | copy-start | bytes 1540
Sparse Core Ops, SparseCore 0:
  46.7 49.0 all-gather.2
  124.7 55.5 all-reduce.6
  185.1 79.0 all-reduce.4
where the time goes:
time: 274 us; the launch traced here: 273 us
  waiting for transfers between devices  149 us (54%)
  blocking collectives  67.9 us (25%)
  matrix products  16.5 us (6%)
  local copies, waits for them, and re-layouts  16.2 us (6%)
  between operations  13.2 us (5%)
  other arithmetic  8.88 us (3%)
    unnamed x4, waiting for transfers between devices  78.6 us
    psum x1, waiting for transfers between devices, shards(): lax.psum((gate_part, upper_part, squares), 'tp')  55.6 us
    all_gather x2, blocking collectives, joined(): pieces = jax.tree.map(lambda part: lax.all_gather(part, axis), value)  34 us
    all_gather x1, blocking collectives, shards(): lax.all_gather(rotated, 'kv', axis=0, tiled=True)  20.5 us
    all_gather x1, waiting for transfers between devices, joined(): pieces = jax.tree.map(lambda part: lax.all_gather(part, axis), value)  15.1 us
    psum x1, blocking collectives, shards(): lax.psum((gate_part, upper_part, squares), 'tp')  13.4 us
  transfers between devices with their start and end apart: 3, of which 3 were waited for; matrix products, arithmetic and copies ran while one was open for 0% of the time, Pallas kernels for 0%

commit v1 on v0

v1 whole, which is shorter than its diff:
```python
from functools import partial

import jax
import jax.numpy as jnp
from jax import lax
from jax.experimental import pallas as pl
from jax.experimental.pallas import tpu as pltpu
from jax.sharding import PartitionSpec as P

fill_value = -1e30
epsilon = 1e-05
f32 = jnp.float32
bf16 = jnp.bfloat16
MESH = pl.DeviceIdType.MESH

KV = 16
TP = 8
HEADS = 16
HD = 128
SLOTS = 4
FEATURES = HEADS * HD
UNITS = 1664
CHUNK = 256
WHOLE = UNITS // CHUNK
TAIL = UNITS - WHOLE * CHUNK
CHUNKS = WHOLE + 1


def dot(left, right):
    return jnp.dot(left, right, preferred_element_type=f32)


def split3(value):
    high = value.astype(bf16).astype(f32)
    rest = value - high
    middle = rest.astype(bf16).astype(f32)
    return high, middle, rest - middle


def in_lanes(parts):
    rows = parts[0].shape[0]
    lane = lax.broadcasted_iota(jnp.int32, (rows, 128), 1)
    tile = jnp.zeros((rows, 128), f32)
    for place, part in enumerate(parts):
        tile = jnp.where(lane == place, part, tile)
    return tile.astype(bf16)


def layer(
    table,
    count,
    queries_hbm,
    signs_hbm,
    keys_hbm,
    values_hbm,
    residual_hbm,
    gain_hbm,
    gate_hbm,
    up_hbm,
    down_hbm,
    out,
    queries,
    signs,
    keys,
    values,
    residual,
    gain,
    gate,
    up,
    down,
    rotated,
    part_out,
    part_in,
    attended,
    stage,
    scaled,
    square_out,
    square_in,
    sums_out,
    sums_in,
    hidden,
    mixed_out,
    mixed_in,
    load_sem,
    send_sem,
    recv_sem,
):
    kv = lax.axis_index("kv")
    tp = lax.axis_index("tp")

    loads = [
        pltpu.make_async_copy(source, target, load_sem.at[place])
        for place, (source, target) in enumerate(
            [
                (queries_hbm, queries),
                (signs_hbm, signs),
                (residual_hbm, residual),
                (gain_hbm, gain),
                (keys_hbm, keys),
                (values_hbm, values),
                (gate_hbm, gate),
                (up_hbm, up),
                (down_hbm, down),
            ]
        )
    ]
    for load in loads:
        load.start()

    barrier = pltpu.get_barrier_semaphore()

    def greet_kv(step, carry):
        pl.semaphore_signal(
            barrier, inc=1, device_id={"kv": lax.rem(kv + step, KV)}, device_id_type=MESH
        )
        return carry

    def greet_tp(step, carry):
        pl.semaphore_signal(
            barrier, inc=1, device_id={"tp": lax.rem(tp + step, TP)}, device_id_type=MESH
        )
        return carry

    lax.fori_loop(1, KV, greet_kv, 0)
    lax.fori_loop(1, TP, greet_tp, 0)

    def to_kv(phase, source, target, peer):
        return pltpu.make_async_remote_copy(
            src_ref=source,
            dst_ref=target,
            send_sem=send_sem.at[phase],
            recv_sem=recv_sem.at[phase],
            device_id={"kv": peer},
            device_id_type=MESH,
        )

    def to_tp(phase, source, target, peer):
        return pltpu.make_async_remote_copy(
            src_ref=source,
            dst_ref=target,
            send_sem=send_sem.at[phase],
            recv_sem=recv_sem.at[phase],
            device_id={"tp": peer},
            device_id_type=MESH,
        )

    def all_kv(phase, buffer):
        return to_kv(phase, buffer.at[pl.ds(0, KV - 1)], buffer.at[pl.ds(0, KV - 1)], kv)

    row = lax.broadcasted_iota(jnp.int32, (HD, HD), 0)
    column = lax.broadcasted_iota(jnp.int32, (HD, HD), 1)
    common = row & column
    parity = common
    for shift in (4, 2, 1):
        parity = parity ^ (parity >> shift)
    turn = ((1 - 2 * (parity & 1)).astype(f32) * (1.0 / HD)).astype(bf16)
    loads[0].wait()
    loads[1].wait()
    wide = queries[...].astype(f32)
    heads = jnp.concatenate(
        [wide[:, head * HD : (head + 1) * HD] for head in range(HEADS)], axis=0
    )
    sign = (1 - 2 * signs[...]).astype(f32)
    rotated[kv] = dot((heads * sign).astype(bf16), turn).astype(bf16)

    pl.semaphore_wait(barrier, KV + TP - 2)

    def send_rotated(step, carry):
        to_kv(0, rotated.at[kv], rotated.at[kv], lax.rem(kv + step, KV)).start()
        return carry

    lax.fori_loop(1, KV, send_rotated, 0)

    loads[2].wait()
    loads[3].wait()
    for head in range(HEADS):
        stage[pl.ds(head, KV, stride=HEADS), :] = residual[:, head * HD : (head + 1) * HD].astype(
            f32
        )
    own_residual = stage[pl.ds(pl.multiple_of(kv * HEADS, HEADS), HEADS), :]

    loads[4].wait()
    loads[5].wait()
    all_kv(0, rotated).wait_recv()

    def attend(request):
        query = rotated[request]
        live = count[0, request]
        pages = [table[0, request, slot] for slot in range(SLOTS)]
        scores = [
            jnp.where(
                slot < live,
                lax.dot_general(
                    query, keys[page], (((1,), (1,)), ((), ())), preferred_element_type=f32
                ),
                fill_value,
            )
            for slot, page in enumerate(pages)
        ]
        best = scores[0]
        for score in scores[1:]:
            best = jnp.maximum(best, score)
        best = jnp.max(best, axis=1, keepdims=True)
        weights = [jnp.exp(score - best).astype(bf16) for score in scores]
        total = weights[0].astype(f32)
        for weight in weights[1:]:
            total = total + weight.astype(f32)
        total = jnp.sum(total, axis=1, keepdims=True)
        merged = dot(weights[0], values[pages[0]])
        for weight, page in zip(weights[1:], pages[1:]):
            merged = merged + dot(weight, values[page])
        part_out[request, :, :HD] = (merged / total).astype(bf16)
        part_out[request, :, HD:] = in_lanes(split3(best + jnp.log(total)))

    def send_part(peer):
        to_kv(1, part_out.at[peer], part_in.at[kv], peer).start()

    def attend_block(block, carry):
        peers = [lax.rem(kv + 1 + block * 4 + place, KV) for place in range(4)]
        for peer in peers:
            attend(peer)
        for peer in peers:
            send_part(peer)
        return carry

    lax.fori_loop(0, 3, attend_block, 0)
    peers = [lax.rem(kv + 13 + place, KV) for place in range(4)]
    for peer in peers:
        attend(peer)
    for peer in peers[:3]:
        send_part(peer)
    part_in[kv] = part_out[kv]

    all_kv(1, part_in).wait_recv()
    level = jnp.sum(part_in[:, :, HD:].astype(f32), axis=2, keepdims=True)
    factor = jnp.exp(level - jnp.max(level, axis=0, keepdims=True))
    whole = jnp.sum(factor * part_in[:, :, :HD].astype(f32), axis=0)
    attention = (whole / jnp.sum(factor, axis=0)).astype(bf16)
    attended[kv] = attention

    def send_attended(step, carry):
        to_kv(2, attended.at[kv], attended.at[kv], lax.rem(kv + step, KV)).start()
        return carry

    lax.fori_loop(1, KV, send_attended, 0)
    own_stream = own_residual + attention.astype(f32)

    all_kv(2, attended).wait_recv()
    stage[...] = attended[...].astype(f32).reshape(KV * HEADS, HD)
    squares = jnp.zeros((KV, HD), f32)
    for head in range(HEADS):
        span = slice(head * HD, (head + 1) * HD)
        piece = residual[:, span].astype(f32) + stage[pl.ds(head, KV, stride=HEADS), :]
        squares = squares + piece * piece
        scaled[:, span] = (piece * gain[:, span].astype(f32)).astype(bf16)
    square_out[...] = in_lanes(split3(jnp.sum(squares, axis=1, keepdims=True)))
    square_in[tp] = square_out[...]

    def send_squares(step, carry):
        to_tp(3, square_out, square_in.at[tp], lax.rem(tp + step, TP)).start()
        return carry

    lax.fori_loop(1, TP, send_squares, 0)

    loads[6].wait()
    loads[7].wait()

    def project(step, carry):
        peer = lax.rem(tp + 1 + step, CHUNKS)

        @pl.when(peer < WHOLE)
        def _():
            span = pl.ds(pl.multiple_of(peer * CHUNK, CHUNK), CHUNK)
            sums_out[peer, :, :CHUNK] = dot(scaled[...], gate[:, span]).astype(bf16)
            sums_out[peer, :, CHUNK:] = dot(scaled[...], up[:, span]).astype(bf16)

            @pl.when(peer != tp)
            def _():
                to_tp(4, sums_out.at[peer], sums_in.at[tp], peer).start()

        @pl.when(peer == WHOLE)
        def _():
            sums_out[WHOLE, :, :TAIL] = dot(scaled[...], gate[:, WHOLE * CHUNK :]).astype(bf16)
            sums_out[WHOLE, :, TAIL : 2 * TAIL] = dot(
                scaled[...], up[:, WHOLE * CHUNK :]
            ).astype(bf16)

            @pl.when(peer != tp)
            def _():
                short = pl.ds(0, 2 * TAIL)
                to_tp(
                    7, sums_out.at[WHOLE, :, short], sums_in.at[tp, :, short], WHOLE
                ).start()

        return carry

    lax.fori_loop(0, CHUNKS, project, 0)

    def all_tp(phase, buffer, size):
        return to_tp(phase, buffer.at[pl.ds(0, size)], buffer.at[pl.ds(0, size)], tp)

    all_tp(3, square_in, TP - 1).wait_recv()
    mean = jnp.sum(jnp.sum(square_in[...].astype(f32), axis=0), axis=1, keepdims=True) / (
        FEATURES * TP
    )
    inverse = lax.rsqrt(mean + epsilon)

    def activate(gate_sum, up_sum):
        value = gate_sum * inverse
        return (value / (1.0 + jnp.exp(-value)) * (up_sum * inverse)).astype(bf16)

    @pl.when(tp < WHOLE)
    def _():
        sums_in[tp] = sums_out[tp]
        all_tp(4, sums_in, TP - 1).wait_recv()
        total = jnp.sum(sums_in[...].astype(f32), axis=0)
        hidden[tp] = activate(total[:, :CHUNK], total[:, CHUNK:])

        def send_hidden(step, carry):
            to_tp(5, hidden.at[tp], hidden.at[tp], lax.rem(tp + step, TP)).start()
            return carry

        lax.fori_loop(1, TP, send_hidden, 0)

    @pl.when(tp == WHOLE)
    def _():
        short = pl.ds(0, 2 * TAIL)
        sums_in[WHOLE, :, : 2 * TAIL] = sums_out[WHOLE, :, : 2 * TAIL]
        to_tp(
            7,
            sums_in.at[pl.ds(0, TP - 1), :, short],
            sums_in.at[pl.ds(0, TP - 1), :, short],
            tp,
        ).wait_recv()
        total = jnp.sum(sums_in[:, :, : 2 * TAIL].astype(f32), axis=0)
        hidden[WHOLE, :, :TAIL] = activate(total[:, :TAIL], total[:, TAIL:])

        def send_hidden(step, carry):
            tail = pl.ds(0, TAIL)
            to_tp(
                8,
                hidden.at[WHOLE, :, tail],
                hidden.at[WHOLE, :, tail],
                lax.rem(tp + step, TP),
            ).start()
            return carry

        lax.fori_loop(1, TP, send_hidden, 0)

    loads[8].wait()

    tail_part = hidden.at[WHOLE, :, pl.ds(0, TAIL)]

    @pl.when(tp < WHOLE)
    def _():
        all_tp(5, hidden, WHOLE - 1).wait_recv()
        to_tp(8, tail_part, tail_part, tp).wait_recv()

    @pl.when(tp == WHOLE)
    def _():
        all_tp(5, hidden, WHOLE).wait_recv()

    @pl.when(tp > WHOLE)
    def _():
        all_tp(5, hidden, WHOLE).wait_recv()
        to_tp(8, tail_part, tail_part, tp).wait_recv()

    units = jnp.concatenate(
        [hidden[chunk] for chunk in range(WHOLE)] + [hidden[WHOLE, :, :TAIL]], axis=1
    )

    def contract(block, carry):
        width = 2 * HD
        result = dot(units, down[:, pl.ds(pl.multiple_of(block * width, width), width)])
        stage[pl.ds(2 * block, KV, stride=HEADS), :] = result[:, :HD]
        stage[pl.ds(2 * block + 1, KV, stride=HEADS), :] = result[:, HD:]
        return carry

    lax.fori_loop(0, HEADS // 2, contract, 0)
    mixed_out[...] = stage[...].astype(bf16).reshape(KV, HEADS, HD)
    mixed_in[kv] = mixed_out[kv]

    def send_mixed(step, carry):
        peer = lax.rem(kv + step, KV)
        to_kv(6, mixed_out.at[peer], mixed_in.at[kv], peer).start()
        return carry

    lax.fori_loop(1, KV, send_mixed, 0)
    all_kv(6, mixed_in).wait_recv()
    out[...] = (own_stream + jnp.sum(mixed_in[...].astype(f32), axis=0)).astype(bf16)

    all_kv(0, rotated).wait_send()
    all_kv(1, part_out).wait_send()
    all_kv(2, attended).wait_send()
    all_tp(3, square_in, TP - 1).wait_send()
    all_kv(6, mixed_out).wait_send()
    tail_sums = sums_out.at[WHOLE, :, pl.ds(0, 2 * TAIL)]

    @pl.when(tp < WHOLE)
    def _():
        all_tp(4, sums_out, WHOLE - 1).wait_send()
        to_tp(7, tail_sums, tail_sums, tp).wait_send()
        all_tp(5, sums_out.at[:, :, pl.ds(0, CHUNK)], TP - 1).wait_send()

    @pl.when(tp == WHOLE)
    def _():
        all_tp(4, sums_out, WHOLE).wait_send()
        all_tp(8, sums_out.at[:, :, pl.ds(0, TAIL)], TP - 1).wait_send()

    @pl.when(tp > WHOLE)
    def _():
        all_tp(4, sums_out, WHOLE).wait_send()
        to_tp(7, tail_sums, tail_sums, tp).wait_send()


def shards(
    queries,
    sign_bits,
    key_pages,
    value_pages,
    page_table,
    page_count,
    residual,
    norm_gain,
    gate_weight,
    up_weight,
    down_weight,
):
    anywhere = pl.BlockSpec(memory_space=pl.ANY)
    scalars = pl.BlockSpec(memory_space=pltpu.SMEM)
    result = pl.pallas_call(
        layer,
        out_shape=jax.ShapeDtypeStruct((HEADS, HD), bf16),
        in_specs=[scalars] * 2 + [anywhere] * 9,
        out_specs=pl.BlockSpec(memory_space=pltpu.VMEM),
        scratch_shapes=[
            pltpu.VMEM(queries.shape, bf16),
            pltpu.VMEM((1, HD), jnp.int32),
            pltpu.VMEM(key_pages.shape, bf16),
            pltpu.VMEM(value_pages.shape, bf16),
            pltpu.VMEM(residual.shape, bf16),
            pltpu.VMEM((1, FEATURES), bf16),
            pltpu.VMEM(gate_weight.shape, bf16),
            pltpu.VMEM(up_weight.shape, bf16),
            pltpu.VMEM(down_weight.shape, bf16),
            pltpu.VMEM((KV, HEADS, HD), bf16),
            pltpu.VMEM((KV, HEADS, 2 * HD), bf16),
            pltpu.VMEM((KV, HEADS, 2 * HD), bf16),
            pltpu.VMEM((KV, HEADS, HD), bf16),
            pltpu.VMEM((KV * HEADS, HD), f32),
            pltpu.VMEM((KV, FEATURES), bf16),
            pltpu.VMEM((KV, 128), bf16),
            pltpu.VMEM((TP, KV, 128), bf16),
            pltpu.VMEM((TP, KV, 2 * CHUNK), bf16),
            pltpu.VMEM((TP, KV, 2 * CHUNK), bf16),
            pltpu.VMEM((CHUNKS, KV, CHUNK), bf16),
            pltpu.VMEM((KV, HEADS, HD), bf16),
            pltpu.VMEM((KV, HEADS, HD), bf16),
            pltpu.SemaphoreType.DMA((9,)),
            pltpu.SemaphoreType.DMA((9,)),
            pltpu.SemaphoreType.DMA((9,)),
        ],
        compiler_params=pltpu.CompilerParams(
            collective_id=0, has_side_effects=True, vmem_limit_bytes=48 * 1024 * 1024
        ),
    )(
        page_table,
        page_count,
        queries,
        sign_bits.reshape(1, HD),
        key_pages,
        value_pages,
        residual,
        norm_gain.reshape(1, FEATURES),
        gate_weight,
        up_weight,
        down_weight,
    )
    return result.reshape(1, FEATURES)


def solution(mesh):
    in_specs = (
        P("kv", "tp"),
        P(),
        P("kv", None, "tp"),
        P("kv", None, "tp"),
        P("kv", None, None),
        P("kv", None),
        P(None, "tp"),
        P("tp"),
        P("tp", "kv"),
        P("tp", "kv"),
        P("kv", "tp"),
    )
    out_specs = P("kv", "tp")
    return jax.shard_map(shards, mesh=mesh, in_specs=in_specs, out_specs=out_specs, check_vma=False)
```

time: 274 us -> 51.4 us (0.19)
  waiting for transfers between devices: 149 us -> 0 us
  blocking collectives: 67.9 us -> 0 us
  Pallas kernels: 0 us -> 43 us
  matrix products: 16.5 us -> 0 us
  between operations: 13.2 us -> 0.02 us
  other arithmetic: 8.88 us -> 0 us
  local copies, waits for them, and re-layouts: 16.2 us -> 8.08 us
    unnamed x4 -> x0, waiting for transfers between devices: 78.6 us -> none
    psum x1 -> x0, waiting for transfers between devices: 55.6 us -> none  [shards(): lax.psum((gate_part, upper_part, squares), 'tp')]
    all_gather x3 -> x0, blocking collectives: 54.5 us -> none  [the longest x2 34 us: joined(): pieces = jax.tree.map(lambda part: lax.all_gather(part, axis), value)]
    pallas_call x0 -> x1, Pallas kernels: none -> 43 us  [shards(): pl.pallas_call(layer, out_shape=jax.ShapeDtypeStruct((HEADS, HD), bf16),...]
    dot_general x8 -> x0, matrix products: 16.5 us -> none  [the longest x1 4.75 us: shards(): jnp.dot(hidden, down_weight, preferred_element_type=jnp.float32)]
    all_gather x1 -> x0, waiting for transfers between devices: 15.1 us -> none  [joined(): pieces = jax.tree.map(lambda part: lax.all_gather(part, axis), value)]
    psum x1 -> x0, blocking collectives: 13.4 us -> none  [shards(): lax.psum((gate_part, upper_part, squares), 'tp')]
    gather x4 -> x0, local copies, waits for them, and re-layouts: 10.2 us -> none  [the longest x2 5.09 us: request_partials(): key_pages[page_list].reshape(slots, key_pages.shape[1], groups, head_size)]
  transfers between devices with their start and end apart: 3 -> 0, of which waited for: 3 -> 0; matrix products, arithmetic and copies ran while one was open for 0% -> 0% of each run, Pallas kernels for 0% -> 0%
where the time goes in v1:
time: 51.4 us; the launch traced here: 51.1 us
  Pallas kernels  43 us (84%)
  local copies, waits for them, and re-layouts  8.08 us (16%)
    pallas_call x1, Pallas kernels, shards(): pl.pallas_call(layer, out_shape=jax.ShapeDtypeStruct((HEADS, HD), bf16),...  43 us
    unnamed x14, local copies, waits for them, and re-layouts  7.39 us

profile of v1, /device:TPU:1, one launch (start us, length us, event | category | flops | bytes accessed | tf_op | source)
XLA Modules:
  0.0 51.1 jit_solution(9590695489024721366)
XLA Ops:
  0.0 0.8 %copy.12.table = s32[1,16,4]{2,1,0:T(8,128)S(1)} copy(s32[1,16,4]{1,2,0:T(4,128)} %param.15) | data formatting | bytes 512 | tf_op args[4]
  0.8 0.7 %reshape.10.gain_hbm = bf16[1,2048]{1,0:T(2,128)(2,1)S(1)} reshape(bf16[2048]{0:T(1024)(128)(2,1)} %param.18) | data formatting | bytes 8192 | tf_op jit(solution)/shard_map/reshape | solution.py:474
  1.5 0.0 copy-start
  1.5 1.6 %copy-done = bf16[32,256,128]{2,1,0:T(8,128)(2,1)S(1)} copy-done((bf16[32,256,128]{2,1,0:T(8,128)(2,1)S(1)}, bf16[32,256,128]{2,1,0:T(8,128)(2,1)}, u32[]{:S(2)}) %copy-start) | copy-done | bytes 2097176
  3.0 0.0 copy-start.1
  3.0 1.6 %copy-done.1 = bf16[32,256,128]{2,1,0:T(8,128)(2,1)S(1)} copy-done((bf16[32,256,128]{2,1,0:T(8,128)(2,1)S(1)}, bf16[32,256,128]{2,1,0:T(8,128)(2,1)}, u32[]{:S(2)}) %copy-start.1) | copy-done | bytes 2097176
  4.6 0.0 copy-start.2
  4.6 0.8 %copy-done.2 = bf16[16,2048]{1,0:T(8,128)(2,1)S(1)} copy-done((bf16[16,2048]{1,0:T(8,128)(2,1)S(1)}, bf16[16,2048]{1,0:T(8,128)(2,1)}, u32[]{:S(2)}) %copy-start.2) | copy-done | bytes 65560
  5.5 0.0 copy-start.3
  5.5 0.7 %copy-done.3 = bf16[1,2048]{1,0:T(2,128)(2,1)S(1)} copy-done((bf16[1,2048]{1,0:T(2,128)(2,1)S(1)}, bf16[1,2048]{1,0:T(2,128)(2,1)}, u32[]{:S(2)}) %copy-start.3) | copy-done | bytes 4120
  6.2 0.0 copy-start.4
  6.2 0.7 %copy-done.4 = s32[1,16]{1,0:T(1,128)S(1)} copy-done((s32[1,16]{1,0:T(1,128)S(1)}, s32[1,16]{1,0:T(1,128)}, u32[]{:S(2)}) %copy-start.4) | copy-done | bytes 88
  6.8 0.0 copy-start.5
  6.8 0.7 %copy-done.5 = s32[128]{0:T(128)S(1)} copy-done((s32[128]{0:T(128)S(1)}, s32[128]{0:T(128)}, u32[]{:S(2)}) %copy-start.5) | copy-done | bytes 536
  7.5 43.0 %shard_map.109 = bf16[16,128]{1,0:T(8,128)(2,1)S(1)} custom-call(s32[1,16,4]{2,1,0:T(8,128)S(1)} %copy.12.table, s32[1,16]{1,0:T(1,128)S(1)} %copy-done.4, bf16[1,2048]{1,0:T(2,128)(2,1)S(1)} %copy-done.3, s32[1,128]{1,0:T(1,128)S(1)} %bitcast.7, bf16[32,256,128]{2,1,0:T(8,128)(2,1)S(1)} %copy-done, bf16[32,256,128]{2,1,0:T(8,128)(2,1)S(1)} %copy-done.1, ...), custom_call_target="tpu_custom_call" | custom-call | tf_op jit(solution)/shard_map/pallas_call | solution.py:431
  50.5 0.6 %copy.15 = bf16[1,1,16,128]{3,1,2,0:T(2,128)(2,1)} copy(bf16[1,1,16,128]{3,2,1,0:T(8,128)(2,1)S(1)} %bitcast.6) | data formatting | bytes 8192
Async XLA Ops:
  1.5 1.6 %copy-start = (bf16[32,256,128]{2,1,0:T(8,128)(2,1)S(1)}, bf16[32,256,128]{2,1,0:T(8,128)(2,1)}, u32[]{:S(2)}) copy-start(bf16[32,256,128]{2,1,0:T(8,128)(2,1)} %keys_hbm.1) | copy-start | bytes 6291460
  3.0 1.6 %copy-start.1 = (bf16[32,256,128]{2,1,0:T(8,128)(2,1)S(1)}, bf16[32,256,128]{2,1,0:T(8,128)(2,1)}, u32[]{:S(2)}) copy-start(bf16[32,256,128]{2,1,0:T(8,128)(2,1)} %values_hbm.1) | copy-start | bytes 6291460
  4.6 0.8 %copy-start.2 = (bf16[16,2048]{1,0:T(8,128)(2,1)S(1)}, bf16[16,2048]{1,0:T(8,128)(2,1)}, u32[]{:S(2)}) copy-start(bf16[16,2048]{1,0:T(8,128)(2,1)} %residual_hbm.1) | copy-start | bytes 196612
  5.5 0.7 %copy-start.3 = (bf16[1,2048]{1,0:T(2,128)(2,1)S(1)}, bf16[1,2048]{1,0:T(2,128)(2,1)}, u32[]{:S(2)}) copy-start(bf16[1,2048]{1,0:T(2,128)(2,1)} %queries_hbm.1) | copy-start | bytes 12292
  6.2 0.7 %copy-start.4 = (s32[1,16]{1,0:T(1,128)S(1)}, s32[1,16]{1,0:T(1,128)}, u32[]{:S(2)}) copy-start(s32[1,16]{1,0:T(1,128)} %count.1) | copy-start | bytes 196
  6.8 0.7 %copy-start.5 = (s32[128]{0:T(128)S(1)}, s32[128]{0:T(128)}, u32[]{:S(2)}) copy-start(s32[128]{0:T(128)} %param.12) | copy-start | bytes 1540

commit v2 on v1

v2 whole, which is shorter than its diff:
```python
from functools import partial

import jax
import jax.numpy as jnp
from jax import lax
from jax.experimental import pallas as pl
from jax.experimental.pallas import tpu as pltpu
from jax.sharding import PartitionSpec as P

fill_value = -1e30
epsilon = 1e-05
f32 = jnp.float32
bf16 = jnp.bfloat16
MESH = pl.DeviceIdType.MESH

KV = 16
TP = 8
HEADS = 16
HD = 128
SLOTS = 4
PAGES = 32
FEATURES = HEADS * HD
UNITS = 1664
CHUNK = 256
CHUNKS = -(-UNITS // CHUNK)
PADDED = CHUNKS * CHUNK


def dot(left, right):
    return jnp.dot(left, right, preferred_element_type=f32)


def split3(value):
    high = value.astype(bf16).astype(f32)
    rest = value - high
    middle = rest.astype(bf16).astype(f32)
    return high, middle, rest - middle


def in_lanes(parts):
    rows = parts[0].shape[0]
    lane = lax.broadcasted_iota(jnp.int32, (rows, 128), 1)
    tile = jnp.zeros((rows, 128), f32)
    for place, part in enumerate(parts):
        tile = jnp.where(lane == place, part, tile)
    return tile.astype(bf16)


def layer(
    table_hbm,
    count_hbm,
    queries_hbm,
    signs_hbm,
    keys_hbm,
    values_hbm,
    residual_hbm,
    gain_hbm,
    gate_hbm,
    up_hbm,
    down_hbm,
    out,
    table,
    count,
    queries,
    signs,
    owner_row,
    owner,
    keys,
    values,
    residual,
    gain,
    gate,
    up,
    down,
    rotated,
    page_max,
    page_total,
    page_out,
    part_out,
    part_in,
    attended,
    stage,
    scaled,
    square_out,
    square_in,
    sums_out,
    sums_in,
    hidden,
    mixed_out,
    mixed_in,
    load_sem,
    send_sem,
    recv_sem,
):
    kv = lax.axis_index("kv")
    tp = lax.axis_index("tp")

    loads = [
        pltpu.make_async_copy(source, target, load_sem.at[place])
        for place, (source, target) in enumerate(
            [
                (queries_hbm, queries),
                (signs_hbm, signs),
                (residual_hbm, residual),
                (gain_hbm, gain),
                (keys_hbm, keys),
                (values_hbm, values),
                (gate_hbm, gate.at[:, pl.ds(0, UNITS)]),
                (up_hbm, up.at[:, pl.ds(0, UNITS)]),
                (down_hbm, down),
                (table_hbm, table),
                (count_hbm, count),
            ]
        )
    ]
    for place in (0, 1, 9, 10, 2, 3, 4, 5, 6, 7, 8):
        loads[place].start()

    x, z = kv // 4, lax.rem(kv, 4)
    offsets = [(dx, dz) for dx in range(4) for dz in range(4) if dx or dz]
    offsets.sort(key=lambda at: -min(at[0], 4 - at[0]) - min(at[1], 4 - at[1]))
    kv_peers = [lax.rem(x + dx, 4) * 4 + lax.rem(z + dz, 4) for dx, dz in offsets]
    tp_peers = [lax.rem(tp + step, TP) for step in (4, 5, 3, 2, 6, 7, 1)]

    barrier = pltpu.get_barrier_semaphore()
    for peer in kv_peers:
        pl.semaphore_signal(barrier, inc=1, device_id={"kv": peer}, device_id_type=MESH)
    for peer in tp_peers:
        pl.semaphore_signal(barrier, inc=1, device_id={"tp": peer}, device_id_type=MESH)

    def to_kv(phase, source, target, peer):
        return pltpu.make_async_remote_copy(
            src_ref=source,
            dst_ref=target,
            send_sem=send_sem.at[phase],
            recv_sem=recv_sem.at[phase],
            device_id={"kv": peer},
            device_id_type=MESH,
        )

    def to_tp(phase, source, target, peer):
        return pltpu.make_async_remote_copy(
            src_ref=source,
            dst_ref=target,
            send_sem=send_sem.at[phase],
            recv_sem=recv_sem.at[phase],
            device_id={"tp": peer},
            device_id_type=MESH,
        )

    def all_kv(phase, buffer):
        return to_kv(phase, buffer.at[pl.ds(0, KV - 1)], buffer.at[pl.ds(0, KV - 1)], kv)

    row = lax.broadcasted_iota(jnp.int32, (HD, HD), 0)
    column = lax.broadcasted_iota(jnp.int32, (HD, HD), 1)
    common = row & column
    parity = common
    for shift in (4, 2, 1):
        parity = parity ^ (parity >> shift)
    turn = ((1 - 2 * (parity & 1)).astype(f32) * (1.0 / HD)).astype(bf16)
    loads[0].wait()
    loads[1].wait()
    wide = queries[...].astype(f32)
    heads = jnp.concatenate(
        [wide[:, head * HD : (head + 1) * HD] for head in range(HEADS)], axis=0
    )
    sign = (1 - 2 * signs[...]).astype(f32)
    rotated[kv] = dot((heads * sign).astype(bf16), turn).astype(bf16)

    loads[9].wait()
    loads[10].wait()
    page_lane = lax.broadcasted_iota(jnp.int32, (1, 128), 1)
    owners = jnp.zeros((1, 128), jnp.int32)
    for request in range(KV):
        for slot in range(SLOTS):
            page = jnp.where(slot < count[0, request], table[0, slot, request], -1)
            owners = jnp.where(page_lane == page, request, owners)
    owner_row[...] = owners
    owner_copy = pltpu.make_async_copy(owner_row, owner, load_sem.at[11])
    owner_copy.start()
    gate[:, UNITS:] = jnp.zeros((FEATURES, PADDED - UNITS), bf16)
    up[:, UNITS:] = jnp.zeros((FEATURES, PADDED - UNITS), bf16)

    pl.semaphore_wait(barrier, KV + TP - 2)

    for peer in kv_peers:
        to_kv(0, rotated.at[kv], rotated.at[kv], peer).start()

    loads[2].wait()
    loads[3].wait()
    for head in range(HEADS):
        stage[pl.ds(head, KV, stride=HEADS), :] = residual[:, head * HD : (head + 1) * HD].astype(
            f32
        )
    own_residual = stage[pl.ds(pl.multiple_of(kv * HEADS, HEADS), HEADS), :]

    owner_copy.wait()
    loads[4].wait()
    loads[5].wait()
    all_kv(0, rotated).wait_recv()

    pages = range(PAGES)
    scores = [
        lax.dot_general(
            rotated[owner[0, page]],
            keys[page],
            (((1,), (1,)), ((), ())),
            preferred_element_type=f32,
        )
        for page in pages
    ]
    largest = [jnp.max(score, axis=1, keepdims=True) for score in scores]
    weights = [jnp.exp(score - best).astype(bf16) for score, best in zip(scores, largest)]
    totals = [jnp.sum(weight.astype(f32), axis=1, keepdims=True) for weight in weights]
    outs = [dot(weight, values[page]) for page, weight in zip(pages, weights)]
    for page in pages:
        page_max[page] = jnp.broadcast_to(largest[page], (HEADS, HD))
        page_total[page] = jnp.broadcast_to(totals[page], (HEADS, HD))
        page_out[page] = outs[page]

    parts = []
    for request in range(KV):
        owned = [table[0, slot, request] for slot in range(SLOTS)]
        live = count[0, request]
        tops = [
            jnp.where(slot < live, page_max[page], fill_value) for slot, page in enumerate(owned)
        ]
        best = jnp.maximum(jnp.maximum(tops[0], tops[1]), jnp.maximum(tops[2], tops[3]))
        factors = [jnp.exp(top - best) for top in tops]
        total = sum(factor * page_total[page] for factor, page in zip(factors, owned))
        merged = sum(factor * page_out[page] for factor, page in zip(factors, owned))
        parts.append(((merged / total).astype(bf16), in_lanes(split3(best + jnp.log(total)))))
    for request, (value, level) in enumerate(parts):
        part_out[request, :, :HD] = value
        part_out[request, :, HD:] = level
    for peer in kv_peers:
        to_kv(1, part_out.at[peer], part_in.at[kv], peer).start()
    part_in[kv] = part_out[kv]

    all_kv(1, part_in).wait_recv()
    level = jnp.sum(part_in[:, :, HD:].astype(f32), axis=2, keepdims=True)
    factor = jnp.exp(level - jnp.max(level, axis=0, keepdims=True))
    whole = jnp.sum(factor * part_in[:, :, :HD].astype(f32), axis=0)
    attention = (whole / jnp.sum(factor, axis=0)).astype(bf16)
    attended[kv] = attention

    for peer in kv_peers:
        to_kv(2, attended.at[kv], attended.at[kv], peer).start()
    own_stream = own_residual + attention.astype(f32)

    all_kv(2, attended).wait_recv()
    stage[...] = attended[...].astype(f32).reshape(KV * HEADS, HD)
    squares = jnp.zeros((KV, HD), f32)
    for head in range(HEADS):
        span = slice(head * HD, (head + 1) * HD)
        piece = residual[:, span].astype(f32) + stage[pl.ds(head, KV, stride=HEADS), :]
        squares = squares + piece * piece
        scaled[:, span] = (piece * gain[span].astype(f32)[None, :]).astype(bf16)
    square_out[...] = in_lanes(split3(jnp.sum(squares, axis=1, keepdims=True)))
    square_in[tp] = square_out[...]

    for peer in tp_peers:
        to_tp(3, square_out, square_in.at[tp], peer).start()

    loads[6].wait()
    loads[7].wait()

    for step in range(CHUNKS):
        peer = lax.rem(tp + 1 + step, CHUNKS)
        span = pl.ds(pl.multiple_of(peer * CHUNK, CHUNK), CHUNK)
        sums_out[peer, :, :CHUNK] = dot(scaled[...], gate[:, span]).astype(bf16)
        sums_out[peer, :, CHUNK:] = dot(scaled[...], up[:, span]).astype(bf16)
        if step < CHUNKS - 1:
            to_tp(4, sums_out.at[peer], sums_in.at[tp], peer).start()

    @pl.when(tp == CHUNKS)
    def _():
        to_tp(4, sums_out.at[0], sums_in.at[tp], 0).start()

    def all_tp(phase, buffer, size):
        return to_tp(phase, buffer.at[pl.ds(0, size)], buffer.at[pl.ds(0, size)], tp)

    all_tp(3, square_in, TP - 1).wait_recv()
    mean = jnp.sum(jnp.sum(square_in[...].astype(f32), axis=0), axis=1, keepdims=True) / (
        FEATURES * TP
    )
    inverse = lax.rsqrt(mean + epsilon)

    def activate(gate_sum, up_sum):
        value = gate_sum * inverse
        return (value / (1.0 + jnp.exp(-value)) * (up_sum * inverse)).astype(bf16)

    @pl.when(tp < CHUNKS)
    def _():
        sums_in[tp] = sums_out[tp]
        all_tp(4, sums_in, TP - 1).wait_recv()
        total = jnp.sum(sums_in[...].astype(f32), axis=0)
        hidden[tp] = activate(total[:, :CHUNK], total[:, CHUNK:])
        for peer in tp_peers:
            to_tp(5, hidden.at[tp], hidden.at[tp], peer).start()

    loads[8].wait()

    @pl.when(tp < CHUNKS)
    def _():
        all_tp(5, hidden, CHUNKS - 1).wait_recv()

    @pl.when(tp == CHUNKS)
    def _():
        all_tp(5, hidden, CHUNKS).wait_recv()

    units = jnp.concatenate([hidden[chunk] for chunk in range(CHUNKS)], axis=1)[:, :UNITS]
    result = dot(units, down[...])
    for head in range(HEADS):
        stage[pl.ds(head, KV, stride=HEADS), :] = result[:, head * HD : (head + 1) * HD]
    mixed_out[...] = stage[...].astype(bf16).reshape(KV, HEADS, HD)
    for peer in kv_peers:
        to_kv(6, mixed_out.at[peer], mixed_in.at[kv], peer).start()
    mixed_in[kv] = mixed_out[kv]
    all_kv(6, mixed_in).wait_recv()
    out[...] = (own_stream + jnp.sum(mixed_in[...].astype(f32), axis=0)).astype(bf16)

    all_kv(0, rotated).wait_send()
    all_kv(1, part_out).wait_send()
    all_kv(2, attended).wait_send()
    all_tp(3, square_in, TP - 1).wait_send()
    all_kv(6, mixed_out).wait_send()

    @pl.when(tp < CHUNKS)
    def _():
        all_tp(4, sums_out, CHUNKS - 1).wait_send()
        all_tp(5, sums_out.at[:, :, pl.ds(0, CHUNK)], TP - 1).wait_send()

    @pl.when(tp == CHUNKS)
    def _():
        all_tp(4, sums_out, CHUNKS).wait_send()


def shards(
    queries,
    sign_bits,
    key_pages,
    value_pages,
    page_table,
    page_count,
    residual,
    norm_gain,
    gate_weight,
    up_weight,
    down_weight,
):
    in_hbm = pl.BlockSpec(memory_space=pltpu.HBM)
    result = pl.pallas_call(
        layer,
        out_shape=jax.ShapeDtypeStruct((HEADS, HD), bf16),
        in_specs=[in_hbm] * 11,
        out_specs=pl.BlockSpec(memory_space=pltpu.VMEM),
        scratch_shapes=[
            pltpu.SMEM((1, SLOTS, KV), jnp.int32),
            pltpu.SMEM((1, KV), jnp.int32),
            pltpu.VMEM(queries.shape, bf16),
            pltpu.VMEM((1, HD), jnp.int32),
            pltpu.VMEM((1, 128), jnp.int32),
            pltpu.SMEM((1, 128), jnp.int32),
            pltpu.VMEM(key_pages.shape, bf16),
            pltpu.VMEM(value_pages.shape, bf16),
            pltpu.VMEM(residual.shape, bf16),
            pltpu.VMEM((FEATURES,), bf16),
            pltpu.VMEM((FEATURES, PADDED), bf16),
            pltpu.VMEM((FEATURES, PADDED), bf16),
            pltpu.VMEM(down_weight.shape, bf16),
            pltpu.VMEM((KV, HEADS, HD), bf16),
            pltpu.VMEM((PAGES, HEADS, HD), f32),
            pltpu.VMEM((PAGES, HEADS, HD), f32),
            pltpu.VMEM((PAGES, HEADS, HD), f32),
            pltpu.VMEM((KV, HEADS, 2 * HD), bf16),
            pltpu.VMEM((KV, HEADS, 2 * HD), bf16),
            pltpu.VMEM((KV, HEADS, HD), bf16),
            pltpu.VMEM((KV * HEADS, HD), f32),
            pltpu.VMEM((KV, FEATURES), bf16),
            pltpu.VMEM((KV, 128), bf16),
            pltpu.VMEM((TP, KV, 128), bf16),
            pltpu.VMEM((CHUNKS, KV, 2 * CHUNK), bf16),
            pltpu.VMEM((TP, KV, 2 * CHUNK), bf16),
            pltpu.VMEM((CHUNKS, KV, CHUNK), bf16),
            pltpu.VMEM((KV, HEADS, HD), bf16),
            pltpu.VMEM((KV, HEADS, HD), bf16),
            pltpu.SemaphoreType.DMA((12,)),
            pltpu.SemaphoreType.DMA((7,)),
            pltpu.SemaphoreType.DMA((7,)),
        ],
        compiler_params=pltpu.CompilerParams(
            collective_id=0, has_side_effects=True, vmem_limit_bytes=63 * 1024 * 1024
        ),
    )(
        jnp.transpose(page_table, (0, 2, 1)),
        page_count,
        queries,
        sign_bits.reshape(1, HD),
        key_pages,
        value_pages,
        residual,
        norm_gain,
        gate_weight,
        up_weight,
        down_weight,
    )
    return result.reshape(1, FEATURES)


def solution(mesh):
    in_specs = (
        P("kv", "tp"),
        P(),
        P("kv", None, "tp"),
        P("kv", None, "tp"),
        P("kv", None, None),
        P("kv", None),
        P(None, "tp"),
        P("tp"),
        P("tp", "kv"),
        P("tp", "kv"),
        P("kv", "tp"),
    )
    out_specs = P("kv", "tp")
    return jax.shard_map(shards, mesh=mesh, in_specs=in_specs, out_specs=out_specs, check_vma=False)
```

time: 51.4 us -> 39.9 us (0.78)
  local copies, waits for them, and re-layouts: 8.08 us -> 1.29 us
  Pallas kernels: 43 us -> 38.4 us
    unnamed x14 -> x1, local copies, waits for them, and re-layouts: 7.39 us -> 1.29 us
    pallas_call x1, Pallas kernels: 43 us -> 38.4 us  [shards(): pl.pallas_call(layer, out_shape=jax.ShapeDtypeStruct((HEADS, HD), bf16),...]
    reshape x1 -> x0, local copies, waits for them, and re-layouts: 0.69 us -> none  [shards(): norm_gain.reshape(1, FEATURES)]
where the time goes in v2:
time: 39.9 us; the launch traced here: 39.7 us
  Pallas kernels  38.4 us (96%)
  local copies, waits for them, and re-layouts  1.29 us (3%)
    pallas_call x1, Pallas kernels, shards(): pl.pallas_call(layer, out_shape=jax.ShapeDtypeStruct((HEADS, HD), bf16),...  38.4 us
    unnamed x1, local copies, waits for them, and re-layouts  1.29 us

profile of v2, /device:TPU:1, one launch (start us, length us, event | category | flops | bytes accessed | tf_op | source)
XLA Modules:
  0.0 39.7 jit_solution(3726727779885524912)
XLA Ops:
  0.0 38.4 %shard_map.109 = bf16[16,128]{1,0:T(8,128)(2,1)} custom-call(s32[1,4,16]{2,1,0:T(4,128)} %bitcast.8, s32[1,16]{1,0:T(1,128)} %count_hbm.1, bf16[1,2048]{1,0:T(2,128)(2,1)} %queries_hbm.1, s32[1,128]{1,0:T(1,128)} %bitcast.9, bf16[32,256,128]{2,1,0:T(8,128)(2,1)} %keys_hbm.1, bf16[32,256,128]{2,1,0:T(8,128)(2,1)} %values_hbm.1, ...), custom_call_target="tpu_custom_call" | custom-call | tf_op jit(solution)/shard_map/pallas_call | solution.py:353
  38.4 1.3 %copy.14 = bf16[1,1,16,128]{3,1,2,0:T(2,128)(2,1)} copy(bf16[1,1,16,128]{3,2,1,0:T(8,128)(2,1)} %bitcast.7) | data formatting | bytes 8192

commit v3 on v2

--- a/solution.py
+++ b/solution.py
@@ -28,6 +28,11 @@
 
 def dot(left, right):
     return jnp.dot(left, right, preferred_element_type=f32)
+
+
+def pair_of(kv):
+    x, z = kv // 4, kv % 4
+    return (x % 2) * 4 + (z + 2 * (x // 2)) % 4, x // 2
 
 
 def split3(value):
@@ -76,6 +81,8 @@
     page_max,
     page_total,
     page_out,
+    level_out,
+    level_in,
     part_out,
     part_in,
     attended,
@@ -120,7 +127,21 @@
     offsets = [(dx, dz) for dx in range(4) for dz in range(4) if dx or dz]
     offsets.sort(key=lambda at: -min(at[0], 4 - at[0]) - min(at[1], 4 - at[1]))
     kv_peers = [lax.rem(x + dx, 4) * 4 + lax.rem(z + dz, 4) for dx, dz in offsets]
-    tp_peers = [lax.rem(tp + step, TP) for step in (4, 5, 3, 2, 6, 7, 1)]
+    pair, member = pair_of(kv)
+    near = [(0, 2), (1, 1), (1, 3), (0, 1), (0, 3), (1, 0), (3, 0)]
+    near_peers = [lax.rem(x + dx, 4) * 4 + lax.rem(z + dz, 4) for dx, dz in near]
+
+    y, core = tp // 2, tp % 2
+    row = [
+        lax.rem(y + dy, 4) * 2 + side
+        for dy in (2, 1, 3, 0)
+        for side in ((core, 1 - core) if dy else (1 - core, core))
+    ]
+    tp_peers = row[:-1]
+    gap = sum(jnp.where(peer == TP - 1, place, 0) for place, peer in enumerate(row))
+    chunk_order = [
+        jnp.where(place < gap, row[place], row[place + 1]) for place in range(CHUNKS)
+    ]
 
     barrier = pltpu.get_barrier_semaphore()
     for peer in kv_peers:
@@ -212,44 +233,76 @@
     largest = [jnp.max(score, axis=1, keepdims=True) for score in scores]
     weights = [jnp.exp(score - best).astype(bf16) for score, best in zip(scores, largest)]
     totals = [jnp.sum(weight.astype(f32), axis=1, keepdims=True) for weight in weights]
-    outs = [dot(weight, values[page]) for page, weight in zip(pages, weights)]
     for page in pages:
         page_max[page] = jnp.broadcast_to(largest[page], (HEADS, HD))
         page_total[page] = jnp.broadcast_to(totals[page], (HEADS, HD))
-        page_out[page] = outs[page]
-
-    parts = []
+
+    lane = lax.broadcasted_iota(jnp.int32, (HEADS, 128), 1)
+    levels = jnp.zeros((HEADS, 128), f32)
+    owned = [[table[0, slot, request] for slot in range(SLOTS)] for request in range(KV)]
+    shares = []
     for request in range(KV):
-        owned = [table[0, slot, request] for slot in range(SLOTS)]
         live = count[0, request]
         tops = [
-            jnp.where(slot < live, page_max[page], fill_value) for slot, page in enumerate(owned)
+            jnp.where(slot < live, page_max[page], fill_value)
+            for slot, page in enumerate(owned[request])
         ]
         best = jnp.maximum(jnp.maximum(tops[0], tops[1]), jnp.maximum(tops[2], tops[3]))
         factors = [jnp.exp(top - best) for top in tops]
-        total = sum(factor * page_total[page] for factor, page in zip(factors, owned))
-        merged = sum(factor * page_out[page] for factor, page in zip(factors, owned))
-        parts.append(((merged / total).astype(bf16), in_lanes(split3(best + jnp.log(total)))))
-    for request, (value, level) in enumerate(parts):
-        part_out[request, :, :HD] = value
-        part_out[request, :, HD:] = level
+        total = sum(factor * page_total[page] for factor, page in zip(factors, owned[request]))
+        shares.append([factor / total for factor in factors])
+        which, place = pair_of(request)
+        for part, value in enumerate(split3(best + jnp.log(total))):
+            levels = jnp.where(lane == part * KV + 2 * which + place, value, levels)
+    level_out[...] = levels.astype(bf16)
     for peer in kv_peers:
-        to_kv(1, part_out.at[peer], part_in.at[kv], peer).start()
-    part_in[kv] = part_out[kv]
-
+        to_kv(7, level_out, level_in.at[kv], peer).start()
+    level_in[kv] = level_out[...]
+
+    outs = [dot(weight, values[page]) for page, weight in zip(pages, weights)]
+    for page in pages:
+        page_out[page] = outs[page]
+    merged = [
+        sum(share * page_out[page] for share, page in zip(shares[request], owned[request]))
+        for request in range(KV)
+    ]
+    for request in range(KV):
+        which, place = pair_of(request)
+        part_out[which, place] = merged[request].astype(bf16)
+    for peer in kv_peers:
+        to_kv(1, part_out.at[pair_of(peer)[0]], part_in.at[kv], peer).start()
+    part_in[kv] = part_out[pair]
+
+    picked_lane = lax.broadcasted_iota(jnp.int32, (128, 2 * HD), 0)
+    picked_column = lax.broadcasted_iota(jnp.int32, (128, 2 * HD), 1)
+    pick = (
+        (picked_lane < 3 * KV)
+        & (lax.rem(picked_lane, KV) == 2 * pair + jnp.where(picked_column < HD, 0, 1))
+    ).astype(f32).astype(bf16)
+    all_kv(7, level_in).wait_recv()
+    level = dot(level_in[...].reshape(KV * HEADS, 128), pick).reshape(KV, HEADS, 2 * HD)
+    factor = jnp.exp(level - jnp.max(level, axis=0, keepdims=True))
+    whole = jnp.sum(factor, axis=0)
+    factor = factor / whole[None]
     all_kv(1, part_in).wait_recv()
-    level = jnp.sum(part_in[:, :, HD:].astype(f32), axis=2, keepdims=True)
-    factor = jnp.exp(level - jnp.max(level, axis=0, keepdims=True))
-    whole = jnp.sum(factor * part_in[:, :, :HD].astype(f32), axis=0)
-    attention = (whole / jnp.sum(factor, axis=0)).astype(bf16)
-    attended[kv] = attention
-
-    for peer in kv_peers:
-        to_kv(2, attended.at[kv], attended.at[kv], peer).start()
+    both = [
+        jnp.sum(factor[:, :, place * HD : (place + 1) * HD] * part_in[:, place].astype(f32), axis=0)
+        for place in range(2)
+    ]
+    for place in range(2):
+        attended[pair, place] = both[place].astype(bf16)
+    for peer in near_peers:
+        to_kv(2, attended.at[pair], attended.at[pair], peer).start()
+    attention = jnp.where(member == 0, both[0], both[1]).astype(bf16)
     own_stream = own_residual + attention.astype(f32)
 
-    all_kv(2, attended).wait_recv()
-    stage[...] = attended[...].astype(f32).reshape(KV * HEADS, HD)
+    def near_kv(phase, buffer):
+        return to_kv(phase, buffer.at[pl.ds(0, 7)], buffer.at[pl.ds(0, 7)], kv)
+
+    near_kv(2, attended).wait_recv()
+    for request in range(KV):
+        which, place = pair_of(request)
+        stage[request * HEADS : (request + 1) * HEADS, :] = attended[which, place].astype(f32)
     squares = jnp.zeros((KV, HD), f32)
     for head in range(HEADS):
         span = slice(head * HD, (head + 1) * HD)
@@ -265,8 +318,7 @@
     loads[6].wait()
     loads[7].wait()
 
-    for step in range(CHUNKS):
-        peer = lax.rem(tp + 1 + step, CHUNKS)
+    for step, peer in enumerate(chunk_order):
         span = pl.ds(pl.multiple_of(peer * CHUNK, CHUNK), CHUNK)
         sums_out[peer, :, :CHUNK] = dot(scaled[...], gate[:, span]).astype(bf16)
         sums_out[peer, :, CHUNK:] = dot(scaled[...], up[:, span]).astype(bf16)
@@ -275,7 +327,7 @@
 
     @pl.when(tp == CHUNKS)
     def _():
-        to_tp(4, sums_out.at[0], sums_in.at[tp], 0).start()
+        to_tp(4, sums_out.at[CHUNKS - 1], sums_in.at[tp], CHUNKS - 1).start()
 
     def all_tp(phase, buffer, size):
         return to_tp(phase, buffer.at[pl.ds(0, size)], buffer.at[pl.ds(0, size)], tp)
@@ -321,8 +373,9 @@
     out[...] = (own_stream + jnp.sum(mixed_in[...].astype(f32), axis=0)).astype(bf16)
 
     all_kv(0, rotated).wait_send()
-    all_kv(1, part_out).wait_send()
-    all_kv(2, attended).wait_send()
+    all_kv(1, part_in).wait_send()
+    near_kv(2, attended).wait_send()
+    all_kv(7, level_in).wait_send()
     all_tp(3, square_in, TP - 1).wait_send()
     all_kv(6, mixed_out).wait_send()
 
@@ -352,7 +405,7 @@
     in_hbm = pl.BlockSpec(memory_space=pltpu.HBM)
     result = pl.pallas_call(
         layer,
-        out_shape=jax.ShapeDtypeStruct((HEADS, HD), bf16),
+        out_shape=pltpu.VMEM((HEADS, HD), bf16),
         in_specs=[in_hbm] * 11,
         out_specs=pl.BlockSpec(memory_space=pltpu.VMEM),
         scratch_shapes=[
@@ -373,9 +426,11 @@
             pltpu.VMEM((PAGES, HEADS, HD), f32),
             pltpu.VMEM((PAGES, HEADS, HD), f32),
             pltpu.VMEM((PAGES, HEADS, HD), f32),
-            pltpu.VMEM((KV, HEADS, 2 * HD), bf16),
-            pltpu.VMEM((KV, HEADS, 2 * HD), bf16),
-            pltpu.VMEM((KV, HEADS, HD), bf16),
+            pltpu.VMEM((HEADS, 128), bf16),
+            pltpu.VMEM((KV, HEADS, 128), bf16),
+            pltpu.VMEM((KV // 2, 2, HEADS, HD), bf16),
+            pltpu.VMEM((KV, 2, HEADS, HD), bf16),
+            pltpu.VMEM((KV // 2, 2, HEADS, HD), bf16),
             pltpu.VMEM((KV * HEADS, HD), f32),
             pltpu.VMEM((KV, FEATURES), bf16),
             pltpu.VMEM((KV, 128), bf16),
@@ -386,8 +441,8 @@
             pltpu.VMEM((KV, HEADS, HD), bf16),
             pltpu.VMEM((KV, HEADS, HD), bf16),
             pltpu.SemaphoreType.DMA((12,)),
-            pltpu.SemaphoreType.DMA((7,)),
-            pltpu.SemaphoreType.DMA((7,)),
+            pltpu.SemaphoreType.DMA((8,)),
+            pltpu.SemaphoreType.DMA((8,)),
         ],
         compiler_params=pltpu.CompilerParams(
             collective_id=0, has_side_effects=True, vmem_limit_bytes=63 * 1024 * 1024

time: 39.9 us -> 38.1 us (0.955)
  Pallas kernels: 38.4 us -> 37.4 us
  local copies, waits for them, and re-layouts: 1.29 us -> 0.61 us
    pallas_call x1, Pallas kernels: 38.4 us -> 37.4 us  [shards(): pl.pallas_call(layer, out_shape=pltpu.VMEM((HEADS, HD), bf16), in_specs=[...]
    unnamed x1, local copies, waits for them, and re-layouts: 1.29 us -> 0.61 us
where the time goes in v3:
time: 38.1 us; the launch traced here: 38 us
  Pallas kernels  37.4 us (98%)
  local copies, waits for them, and re-layouts  0.61 us (2%)
    pallas_call x1, Pallas kernels, shards(): pl.pallas_call(layer, out_shape=pltpu.VMEM((HEADS, HD), bf16), in_specs=[...  37.4 us

profile of v3, /device:TPU:1, one launch (start us, length us, event | category | flops | bytes accessed | tf_op | source)
XLA Modules:
  0.0 38.0 jit_solution(5968147036493859431)
XLA Ops:
  0.0 37.4 %shard_map.109 = bf16[16,128]{1,0:T(8,128)(2,1)S(1)} custom-call(s32[1,4,16]{2,1,0:T(4,128)} %bitcast.8, s32[1,16]{1,0:T(1,128)} %count_hbm.1, bf16[1,2048]{1,0:T(2,128)(2,1)} %queries_hbm.1, s32[1,128]{1,0:T(1,128)} %bitcast.9, bf16[32,256,128]{2,1,0:T(8,128)(2,1)} %keys_hbm.1, bf16[32,256,128]{2,1,0:T(8,128)(2,1)} %values_hbm.1, ...), custom_call_target="tpu_custom_call" | custom-call | tf_op jit(solution)/shard_map/pallas_call | solution.py:406
  37.4 0.6 %copy.14 = bf16[1,1,16,128]{3,1,2,0:T(2,128)(2,1)} copy(bf16[1,1,16,128]{3,2,1,0:T(8,128)(2,1)S(1)} %bitcast.7) | data formatting | bytes 8192

commit v4 on v3

--- a/solution.py
+++ b/solution.py
@@ -93,6 +93,7 @@
     sums_out,
     sums_in,
     hidden,
+    product,
     mixed_out,
     mixed_in,
     load_sem,
@@ -114,21 +115,21 @@
                 (values_hbm, values),
                 (gate_hbm, gate.at[:, pl.ds(0, UNITS)]),
                 (up_hbm, up.at[:, pl.ds(0, UNITS)]),
-                (down_hbm, down),
+                (down_hbm, down.at[pl.ds(0, UNITS)]),
                 (table_hbm, table),
                 (count_hbm, count),
             ]
         )
     ]
-    for place in (0, 1, 9, 10, 2, 3, 4, 5, 6, 7, 8):
-        loads[place].start()
+    loads[0].start()
+    loads[1].start()
 
     x, z = kv // 4, lax.rem(kv, 4)
     offsets = [(dx, dz) for dx in range(4) for dz in range(4) if dx or dz]
     offsets.sort(key=lambda at: -min(at[0], 4 - at[0]) - min(at[1], 4 - at[1]))
     kv_peers = [lax.rem(x + dx, 4) * 4 + lax.rem(z + dz, 4) for dx, dz in offsets]
     pair, member = pair_of(kv)
-    near = [(0, 2), (1, 1), (1, 3), (0, 1), (0, 3), (1, 0), (3, 0)]
+    near = [(0, 2), (1, 1), (3, 1), (0, 1), (0, 3), (1, 0), (3, 0)]
     near_peers = [lax.rem(x + dx, 4) * 4 + lax.rem(z + dz, 4) for dx, dz in near]
 
     y, core = tp // 2, tp % 2
@@ -148,6 +149,9 @@
         pl.semaphore_signal(barrier, inc=1, device_id={"kv": peer}, device_id_type=MESH)
     for peer in tp_peers:
         pl.semaphore_signal(barrier, inc=1, device_id={"tp": peer}, device_id_type=MESH)
+
+    for place in (9, 10, 2, 3, 4, 5, 6, 7, 8):
+        loads[place].start()
 
     def to_kv(phase, source, target, peer):
         return pltpu.make_async_remote_copy(
@@ -188,6 +192,11 @@
     sign = (1 - 2 * signs[...]).astype(f32)
     rotated[kv] = dot((heads * sign).astype(bf16), turn).astype(bf16)
 
+    pl.semaphore_wait(barrier, KV + TP - 2)
+
+    for peer in kv_peers:
+        to_kv(0, rotated.at[kv], rotated.at[kv], peer).start()
+
     loads[9].wait()
     loads[10].wait()
     page_lane = lax.broadcasted_iota(jnp.int32, (1, 128), 1)
@@ -201,11 +210,7 @@
     owner_copy.start()
     gate[:, UNITS:] = jnp.zeros((FEATURES, PADDED - UNITS), bf16)
     up[:, UNITS:] = jnp.zeros((FEATURES, PADDED - UNITS), bf16)
-
-    pl.semaphore_wait(barrier, KV + TP - 2)
-
-    for peer in kv_peers:
-        to_kv(0, rotated.at[kv], rotated.at[kv], peer).start()
+    down[UNITS:, :] = jnp.zeros((TP * CHUNK - UNITS, FEATURES), bf16)
 
     loads[2].wait()
     loads[3].wait()
@@ -348,21 +353,29 @@
         all_tp(4, sums_in, TP - 1).wait_recv()
         total = jnp.sum(sums_in[...].astype(f32), axis=0)
         hidden[tp] = activate(total[:, :CHUNK], total[:, CHUNK:])
-        for peer in tp_peers:
-            to_tp(5, hidden.at[tp], hidden.at[tp], peer).start()
-
-    loads[8].wait()
-
-    @pl.when(tp < CHUNKS)
-    def _():
-        all_tp(5, hidden, CHUNKS - 1).wait_recv()
 
     @pl.when(tp == CHUNKS)
     def _():
-        all_tp(5, hidden, CHUNKS).wait_recv()
-
-    units = jnp.concatenate([hidden[chunk] for chunk in range(CHUNKS)], axis=1)[:, :UNITS]
-    result = dot(units, down[...])
+        hidden[CHUNKS] = jnp.zeros((KV, CHUNK), bf16)
+
+    for peer in tp_peers[:2]:
+        to_tp(5, hidden.at[tp], hidden.at[tp], peer).start()
+    for peer in tp_peers[2:6]:
+        to_tp(8, hidden.at[tp], hidden.at[tp], peer).start()
+    sibling = tp_peers[6]
+    to_tp(9, hidden.at[tp], hidden.at[tp], sibling).start()
+
+    def chip_product(chip):
+        units = jnp.concatenate([hidden[2 * chip], hidden[2 * chip + 1]], axis=1)
+        return dot(units, down[pl.ds(pl.multiple_of(chip * 2 * CHUNK, 2 * CHUNK), 2 * CHUNK), :])
+
+    loads[8].wait()
+    to_tp(9, hidden.at[sibling], hidden.at[sibling], sibling).wait_recv()
+    product[...] = chip_product(y)
+    all_tp(8, hidden, 4).wait_recv()
+    product[...] += chip_product(lax.rem(y + 1, 4)) + chip_product(lax.rem(y + 3, 4))
+    all_tp(5, hidden, 2).wait_recv()
+    result = product[...] + chip_product(lax.rem(y + 2, 4))
     for head in range(HEADS):
         stage[pl.ds(head, KV, stride=HEADS), :] = result[:, head * HD : (head + 1) * HD]
     mixed_out[...] = stage[...].astype(bf16).reshape(KV, HEADS, HD)
@@ -378,11 +391,13 @@
     all_kv(7, level_in).wait_send()
     all_tp(3, square_in, TP - 1).wait_send()
     all_kv(6, mixed_out).wait_send()
+    all_tp(5, hidden, 2).wait_send()
+    all_tp(8, hidden, 4).wait_send()
+    all_tp(9, hidden, 1).wait_send()
 
     @pl.when(tp < CHUNKS)
     def _():
         all_tp(4, sums_out, CHUNKS - 1).wait_send()
-        all_tp(5, sums_out.at[:, :, pl.ds(0, CHUNK)], TP - 1).wait_send()
 
     @pl.when(tp == CHUNKS)
     def _():
@@ -421,7 +436,7 @@
             pltpu.VMEM((FEATURES,), bf16),
             pltpu.VMEM((FEATURES, PADDED), bf16),
             pltpu.VMEM((FEATURES, PADDED), bf16),
-            pltpu.VMEM(down_weight.shape, bf16),
+            pltpu.VMEM((TP * CHUNK, FEATURES), bf16),
             pltpu.VMEM((KV, HEADS, HD), bf16),
             pltpu.VMEM((PAGES, HEADS, HD), f32),
             pltpu.VMEM((PAGES, HEADS, HD), f32),
@@ -437,12 +452,13 @@
             pltpu.VMEM((TP, KV, 128), bf16),
             pltpu.VMEM((CHUNKS, KV, 2 * CHUNK), bf16),
             pltpu.VMEM((TP, KV, 2 * CHUNK), bf16),
-            pltpu.VMEM((CHUNKS, KV, CHUNK), bf16),
+            pltpu.VMEM((TP, KV, CHUNK), bf16),
+            pltpu.VMEM((KV, FEATURES), f32),
             pltpu.VMEM((KV, HEADS, HD), bf16),
             pltpu.VMEM((KV, HEADS, HD), bf16),
             pltpu.SemaphoreType.DMA((12,)),
-            pltpu.SemaphoreType.DMA((8,)),
-            pltpu.SemaphoreType.DMA((8,)),
+            pltpu.SemaphoreType.DMA((10,)),
+            pltpu.SemaphoreType.DMA((10,)),
         ],
         compiler_params=pltpu.CompilerParams(
             collective_id=0, has_side_effects=True, vmem_limit_bytes=63 * 1024 * 1024

time: 38.1 us -> 37.5 us (0.984)
  Pallas kernels: 37.4 us -> 36.7 us
    pallas_call x1, Pallas kernels: 37.4 us -> 36.7 us  [shards(): pl.pallas_call(layer, out_shape=pltpu.VMEM((HEADS, HD), bf16), in_specs=[...]
where the time goes in v4:
time: 37.5 us; the launch traced here: 37.3 us
  Pallas kernels  36.7 us (98%)
  local copies, waits for them, and re-layouts  0.61 us (2%)
    pallas_call x1, Pallas kernels, shards(): pl.pallas_call(layer, out_shape=pltpu.VMEM((HEADS, HD), bf16), in_specs=[...  36.7 us

profile of v4, /device:TPU:1, one launch (start us, length us, event | category | flops | bytes accessed | tf_op | source)
XLA Modules:
  0.0 37.3 jit_solution(17548983424379896543)
XLA Ops:
  0.0 36.7 %shard_map.109 = bf16[16,128]{1,0:T(8,128)(2,1)S(1)} custom-call(s32[1,4,16]{2,1,0:T(4,128)} %bitcast.8, s32[1,16]{1,0:T(1,128)} %count_hbm.1, bf16[1,2048]{1,0:T(2,128)(2,1)} %queries_hbm.1, s32[1,128]{1,0:T(1,128)} %bitcast.9, bf16[32,256,128]{2,1,0:T(8,128)(2,1)} %keys_hbm.1, bf16[32,256,128]{2,1,0:T(8,128)(2,1)} %values_hbm.1, ...), custom_call_target="tpu_custom_call" | custom-call | tf_op jit(solution)/shard_map/pallas_call | solution.py:421
  36.7 0.6 %copy.14 = bf16[1,1,16,128]{3,1,2,0:T(2,128)(2,1)} copy(bf16[1,1,16,128]{3,2,1,0:T(8,128)(2,1)S(1)} %bitcast.7) | data formatting | bytes 8192

commit v5 on v4

--- a/solution.py
+++ b/solution.py
@@ -81,8 +81,6 @@
     page_max,
     page_total,
     page_out,
-    level_out,
-    level_in,
     part_out,
     part_in,
     attended,
@@ -259,11 +257,9 @@
         which, place = pair_of(request)
         for part, value in enumerate(split3(best + jnp.log(total))):
             levels = jnp.where(lane == part * KV + 2 * which + place, value, levels)
-    level_out[...] = levels.astype(bf16)
-    for peer in kv_peers:
-        to_kv(7, level_out, level_in.at[kv], peer).start()
-    level_in[kv] = level_out[...]
-
+    level_tile = levels.astype(bf16)
+    for which in range(KV // 2):
+        part_out[which, 2] = level_tile
     outs = [dot(weight, values[page]) for page, weight in zip(pages, weights)]
     for page in pages:
         page_out[page] = outs[page]
@@ -284,12 +280,11 @@
         (picked_lane < 3 * KV)
         & (lax.rem(picked_lane, KV) == 2 * pair + jnp.where(picked_column < HD, 0, 1))
     ).astype(f32).astype(bf16)
-    all_kv(7, level_in).wait_recv()
-    level = dot(level_in[...].reshape(KV * HEADS, 128), pick).reshape(KV, HEADS, 2 * HD)
+    all_kv(1, part_in).wait_recv()
+    level = dot(part_in[:, 2].reshape(KV * HEADS, 128), pick).reshape(KV, HEADS, 2 * HD)
     factor = jnp.exp(level - jnp.max(level, axis=0, keepdims=True))
     whole = jnp.sum(factor, axis=0)
     factor = factor / whole[None]
-    all_kv(1, part_in).wait_recv()
     both = [
         jnp.sum(factor[:, :, place * HD : (place + 1) * HD] * part_in[:, place].astype(f32), axis=0)
         for place in range(2)
@@ -317,9 +312,6 @@
     square_out[...] = in_lanes(split3(jnp.sum(squares, axis=1, keepdims=True)))
     square_in[tp] = square_out[...]
 
-    for peer in tp_peers:
-        to_tp(3, square_out, square_in.at[tp], peer).start()
-
     loads[6].wait()
     loads[7].wait()
 
@@ -329,6 +321,9 @@
         sums_out[peer, :, CHUNK:] = dot(scaled[...], up[:, span]).astype(bf16)
         if step < CHUNKS - 1:
             to_tp(4, sums_out.at[peer], sums_in.at[tp], peer).start()
+        if step == 1:
+            for target in tp_peers:
+                to_tp(3, square_out, square_in.at[tp], target).start()
 
     @pl.when(tp == CHUNKS)
     def _():
@@ -388,7 +383,6 @@
     all_kv(0, rotated).wait_send()
     all_kv(1, part_in).wait_send()
     near_kv(2, attended).wait_send()
-    all_kv(7, level_in).wait_send()
     all_tp(3, square_in, TP - 1).wait_send()
     all_kv(6, mixed_out).wait_send()
     all_tp(5, hidden, 2).wait_send()
@@ -441,10 +435,8 @@
             pltpu.VMEM((PAGES, HEADS, HD), f32),
             pltpu.VMEM((PAGES, HEADS, HD), f32),
             pltpu.VMEM((PAGES, HEADS, HD), f32),
-            pltpu.VMEM((HEADS, 128), bf16),
-            pltpu.VMEM((KV, HEADS, 128), bf16),
-            pltpu.VMEM((KV // 2, 2, HEADS, HD), bf16),
-            pltpu.VMEM((KV, 2, HEADS, HD), bf16),
+            pltpu.VMEM((KV // 2, 3, HEADS, HD), bf16),
+            pltpu.VMEM((KV, 3, HEADS, HD), bf16),
             pltpu.VMEM((KV // 2, 2, HEADS, HD), bf16),
             pltpu.VMEM((KV * HEADS, HD), f32),
             pltpu.VMEM((KV, FEATURES), bf16),

time: 37.5 us -> 37.3 us (level)
  no operation moved by 1% of the time
where the time goes in v5:
time: 37.3 us; the launch traced here: 37.2 us
  Pallas kernels  36.6 us (98%)
  local copies, waits for them, and re-layouts  0.61 us (2%)
    pallas_call x1, Pallas kernels, shards(): pl.pallas_call(layer, out_shape=pltpu.VMEM((HEADS, HD), bf16), in_specs=[...  36.6 us

profile of v5, /device:TPU:1, one launch (start us, length us, event | category | flops | bytes accessed | tf_op | source)
XLA Modules:
  0.0 37.2 jit_solution(52290931350786949)
XLA Ops:
  0.0 36.6 %shard_map.109 = bf16[16,128]{1,0:T(8,128)(2,1)S(1)} custom-call(s32[1,4,16]{2,1,0:T(4,128)} %bitcast.8, s32[1,16]{1,0:T(1,128)} %count_hbm.1, bf16[1,2048]{1,0:T(2,128)(2,1)} %queries_hbm.1, s32[1,128]{1,0:T(1,128)} %bitcast.9, bf16[32,256,128]{2,1,0:T(8,128)(2,1)} %keys_hbm.1, bf16[32,256,128]{2,1,0:T(8,128)(2,1)} %values_hbm.1, ...), custom_call_target="tpu_custom_call" | custom-call | tf_op jit(solution)/shard_map/pallas_call | solution.py:415
  36.6 0.6 %copy.14 = bf16[1,1,16,128]{3,1,2,0:T(2,128)(2,1)} copy(bf16[1,1,16,128]{3,2,1,0:T(8,128)(2,1)S(1)} %bitcast.7) | data formatting | bytes 8192

commit v6 on v5

--- a/solution.py
+++ b/solution.py
@@ -133,7 +133,7 @@
     y, core = tp // 2, tp % 2
     row = [
         lax.rem(y + dy, 4) * 2 + side
-        for dy in (2, 1, 3, 0)
+        for dy in (2, 3, 1, 0)
         for side in ((core, 1 - core) if dy else (1 - core, core))
     ]
     tp_peers = row[:-1]
@@ -253,7 +253,8 @@
         best = jnp.maximum(jnp.maximum(tops[0], tops[1]), jnp.maximum(tops[2], tops[3]))
         factors = [jnp.exp(top - best) for top in tops]
         total = sum(factor * page_total[page] for factor, page in zip(factors, owned[request]))
-        shares.append([factor / total for factor in factors])
+        inverse_total = 1.0 / total
+        shares.append([factor * inverse_total for factor in factors])
         which, place = pair_of(request)
         for part, value in enumerate(split3(best + jnp.log(total))):
             levels = jnp.where(lane == part * KV + 2 * which + place, value, levels)
@@ -284,9 +285,10 @@
     level = dot(part_in[:, 2].reshape(KV * HEADS, 128), pick).reshape(KV, HEADS, 2 * HD)
     factor = jnp.exp(level - jnp.max(level, axis=0, keepdims=True))
     whole = jnp.sum(factor, axis=0)
-    factor = factor / whole[None]
+    inverse_whole = 1.0 / whole
     both = [
         jnp.sum(factor[:, :, place * HD : (place + 1) * HD] * part_in[:, place].astype(f32), axis=0)
+        * inverse_whole[:, place * HD : (place + 1) * HD]
         for place in range(2)
     ]
     for place in range(2):
@@ -378,7 +380,9 @@
         to_kv(6, mixed_out.at[peer], mixed_in.at[kv], peer).start()
     mixed_in[kv] = mixed_out[kv]
     all_kv(6, mixed_in).wait_recv()
-    out[...] = (own_stream + jnp.sum(mixed_in[...].astype(f32), axis=0)).astype(bf16)
+    final = own_stream + jnp.sum(mixed_in[...].astype(f32), axis=0)
+    for head in range(HEADS):
+        out[:, head * HD : (head + 1) * HD] = final[head : head + 1].astype(bf16)
 
     all_kv(0, rotated).wait_send()
     all_kv(1, part_in).wait_send()
@@ -414,7 +418,7 @@
     in_hbm = pl.BlockSpec(memory_space=pltpu.HBM)
     result = pl.pallas_call(
         layer,
-        out_shape=pltpu.VMEM((HEADS, HD), bf16),
+        out_shape=pltpu.VMEM((1, FEATURES), bf16),
         in_specs=[in_hbm] * 11,
         out_specs=pl.BlockSpec(memory_space=pltpu.VMEM),
         scratch_shapes=[
@@ -468,7 +472,7 @@
         up_weight,
         down_weight,
     )
-    return result.reshape(1, FEATURES)
+    return result
 
 
 def solution(mesh):

time: 37.3 us -> 37.3 us (level)
  no operation moved by 1% of the time
where the time goes in v6:
time: 37.3 us; the launch traced here: 37.1 us
  Pallas kernels  36.5 us (98%)
  local copies, waits for them, and re-layouts  0.6 us (2%)
    pallas_call x1, Pallas kernels, shards(): pl.pallas_call(layer, out_shape=pltpu.VMEM((1, FEATURES), bf16), in_specs...  36.5 us

profile of v6, /device:TPU:1, one launch (start us, length us, event | category | flops | bytes accessed | tf_op | source)
XLA Modules:
  0.0 37.1 jit_solution(16401296276644860588)
XLA Ops:
  0.0 36.5 %shard_map.109 = bf16[1,2048]{1,0:T(2,128)(2,1)S(1)} custom-call(s32[1,4,16]{2,1,0:T(4,128)} %bitcast.2, s32[1,16]{1,0:T(1,128)} %count_hbm.1, bf16[1,2048]{1,0:T(2,128)(2,1)} %queries_hbm.1, s32[1,128]{1,0:T(1,128)} %bitcast.3, bf16[32,256,128]{2,1,0:T(8,128)(2,1)} %keys_hbm.1, bf16[32,256,128]{2,1,0:T(8,128)(2,1)} %values_hbm.1, ...), custom_call_target="tpu_custom_call" | custom-call | tf_op jit(solution)/shard_map/pallas_call | solution.py:419
  36.5 0.6 %copy.13 = bf16[1,2048]{1,0:T(2,128)(2,1)} copy(bf16[1,2048]{1,0:T(2,128)(2,1)S(1)} %shard_map.109) | data formatting | bytes 8192

commit v7 on v6

--- a/solution.py
+++ b/solution.py
@@ -86,8 +86,6 @@
     attended,
     stage,
     scaled,
-    square_out,
-    square_in,
     sums_out,
     sums_in,
     hidden,
@@ -311,8 +309,7 @@
         piece = residual[:, span].astype(f32) + stage[pl.ds(head, KV, stride=HEADS), :]
         squares = squares + piece * piece
         scaled[:, span] = (piece * gain[span].astype(f32)[None, :]).astype(bf16)
-    square_out[...] = in_lanes(split3(jnp.sum(squares, axis=1, keepdims=True)))
-    square_in[tp] = square_out[...]
+    square_tile = in_lanes(split3(jnp.sum(squares, axis=1, keepdims=True)))
 
     loads[6].wait()
     loads[7].wait()
@@ -320,12 +317,10 @@
     for step, peer in enumerate(chunk_order):
         span = pl.ds(pl.multiple_of(peer * CHUNK, CHUNK), CHUNK)
         sums_out[peer, :, :CHUNK] = dot(scaled[...], gate[:, span]).astype(bf16)
-        sums_out[peer, :, CHUNK:] = dot(scaled[...], up[:, span]).astype(bf16)
+        sums_out[peer, :, CHUNK : 2 * CHUNK] = dot(scaled[...], up[:, span]).astype(bf16)
+        sums_out[peer, :, 2 * CHUNK :] = square_tile
         if step < CHUNKS - 1:
             to_tp(4, sums_out.at[peer], sums_in.at[tp], peer).start()
-        if step == 1:
-            for target in tp_peers:
-                to_tp(3, square_out, square_in.at[tp], target).start()
 
     @pl.when(tp == CHUNKS)
     def _():
@@ -333,23 +328,18 @@
 
     def all_tp(phase, buffer, size):
         return to_tp(phase, buffer.at[pl.ds(0, size)], buffer.at[pl.ds(0, size)], tp)
-
-    all_tp(3, square_in, TP - 1).wait_recv()
-    mean = jnp.sum(jnp.sum(square_in[...].astype(f32), axis=0), axis=1, keepdims=True) / (
-        FEATURES * TP
-    )
-    inverse = lax.rsqrt(mean + epsilon)
-
-    def activate(gate_sum, up_sum):
-        value = gate_sum * inverse
-        return (value / (1.0 + jnp.exp(-value)) * (up_sum * inverse)).astype(bf16)
 
     @pl.when(tp < CHUNKS)
     def _():
         sums_in[tp] = sums_out[tp]
         all_tp(4, sums_in, TP - 1).wait_recv()
         total = jnp.sum(sums_in[...].astype(f32), axis=0)
-        hidden[tp] = activate(total[:, :CHUNK], total[:, CHUNK:])
+        mean = jnp.sum(total[:, 2 * CHUNK :], axis=1, keepdims=True) / (FEATURES * TP)
+        inverse = lax.rsqrt(mean + epsilon)
+        value = total[:, :CHUNK] * inverse
+        hidden[tp] = (
+            value / (1.0 + jnp.exp(-value)) * (total[:, CHUNK : 2 * CHUNK] * inverse)
+        ).astype(bf16)
 
     @pl.when(tp == CHUNKS)
     def _():
@@ -387,7 +377,6 @@
     all_kv(0, rotated).wait_send()
     all_kv(1, part_in).wait_send()
     near_kv(2, attended).wait_send()
-    all_tp(3, square_in, TP - 1).wait_send()
     all_kv(6, mixed_out).wait_send()
     all_tp(5, hidden, 2).wait_send()
     all_tp(8, hidden, 4).wait_send()
@@ -444,10 +433,8 @@
             pltpu.VMEM((KV // 2, 2, HEADS, HD), bf16),
             pltpu.VMEM((KV * HEADS, HD), f32),
             pltpu.VMEM((KV, FEATURES), bf16),
-            pltpu.VMEM((KV, 128), bf16),
-            pltpu.VMEM((TP, KV, 128), bf16),
-            pltpu.VMEM((CHUNKS, KV, 2 * CHUNK), bf16),
-            pltpu.VMEM((TP, KV, 2 * CHUNK), bf16),
+            pltpu.VMEM((CHUNKS, KV, 2 * CHUNK + 128), bf16),
+            pltpu.VMEM((TP, KV, 2 * CHUNK + 128), bf16),
             pltpu.VMEM((TP, KV, CHUNK), bf16),
             pltpu.VMEM((KV, FEATURES), f32),
             pltpu.VMEM((KV, HEADS, HD), bf16),

time: 37.3 us -> 37.4 us (level)
  no operation moved by 1% of the time
where the time goes in v7:
time: 37.4 us; the launch traced here: 37.2 us
  Pallas kernels  36.6 us (98%)
  local copies, waits for them, and re-layouts  0.6 us (2%)
    pallas_call x1, Pallas kernels, shards(): pl.pallas_call(layer, out_shape=pltpu.VMEM((1, FEATURES), bf16), in_specs...  36.6 us

profile of v7, /device:TPU:1, one launch (start us, length us, event | category | flops | bytes accessed | tf_op | source)
XLA Modules:
  0.0 37.2 jit_solution(3285668410613790506)
XLA Ops:
  0.0 36.6 %shard_map.109 = bf16[1,2048]{1,0:T(2,128)(2,1)S(1)} custom-call(s32[1,4,16]{2,1,0:T(4,128)} %bitcast.2, s32[1,16]{1,0:T(1,128)} %count_hbm.1, bf16[1,2048]{1,0:T(2,128)(2,1)} %queries_hbm.1, s32[1,128]{1,0:T(1,128)} %bitcast.3, bf16[32,256,128]{2,1,0:T(8,128)(2,1)} %keys_hbm.1, bf16[32,256,128]{2,1,0:T(8,128)(2,1)} %values_hbm.1, ...), custom_call_target="tpu_custom_call" | custom-call | tf_op jit(solution)/shard_map/pallas_call | solution.py:408
  36.6 0.6 %copy.13 = bf16[1,2048]{1,0:T(2,128)(2,1)} copy(bf16[1,2048]{1,0:T(2,128)(2,1)S(1)} %shard_map.109) | data formatting | bytes 8192
